TPU v7x, 32 devices: a whole 2x2x4 slice. The times are simulated.
32 devices in a mesh: dp: 8 (over z, y), mp: 4 (over x, core).
Axes of the slice: x: 2, y: 2, z: 4, core: 2. Of those that a mesh axis runs over, the one named last changes fastest.
Arguments:
- features_in: bfloat16 [16, 24576], P(None, 'dp'), may hold values from -6 to 6
- w_in: bfloat16 [16, 1024], P(None, 'mp'), may hold values from -1.5 to 1.5
- w_mid: bfloat16 [1024, 1024], P(None, 'mp'), may hold values from -0.1875 to 0.1875
- w_out: bfloat16 [1024], P('mp'), may hold values from -0.1875 to 0.1875
- targets: float32 [24576], P('dp'), may hold values from -6 to 6
- valid_steps: int32 [256], P('dp'), may hold values from 16 to 96, as said below
Outputs:
- predicted_change: float32 [24576], P('dp')
Inputs may be any that keep to these rules, and one draw needn't show every extreme that they name: `valid_steps`: the last building has all 96 valid steps.
All inputs are finite; a program needn't handle non-finite values.
Results may differ from a plain program's by a relative error of at most 0.00037.
Values may be sent and summed in bfloat16 or wider, within the bound.
A program may use at most 64 MiB of HBM per device.

v0:
```python
import jax
import jax.numpy as jnp
from jax import lax
from jax.sharding import PartitionSpec as P

STEPS = 96
ITERS = 3
damping = 0.002


def pull_back(columns, back):
    return lax.dot_general(
        columns, back, (((0,), (0,)), ((), ())), preferred_element_type=jnp.float32
    )


def shards(features_in, w_in, w_mid, w_out, targets, valid_steps):
    out_weight = w_out.astype(jnp.float32)
    valid_count = lax.psum(jnp.sum(valid_steps).astype(jnp.float32), "dp")
    whole_input = lax.all_gather(w_in, "mp", axis=1, tiled=True)
    hidden_one = jnp.tanh(
        jnp.dot(features_in.T, whole_input, preferred_element_type=jnp.float32)
    ).astype(jnp.bfloat16)
    hidden_two = jnp.tanh(jnp.dot(hidden_one, w_mid, preferred_element_type=jnp.float32))
    slope_out = (1.0 - hidden_two * hidden_two) * out_weight
    predicted = lax.psum(jnp.sum(hidden_two * out_weight, axis=-1), "mp")
    step_mask = (
        (jnp.arange(STEPS, dtype=jnp.int32)[None, :] < valid_steps[:, None])
        .astype(jnp.float32)
        .reshape(-1)
    )
    row_weight = step_mask / valid_count
    error_rows = row_weight * (predicted - targets)
    grad_back = (error_rows[:, None] * slope_out).astype(jnp.bfloat16)

    def tangent(dir_bf16):
        partial_rows = jnp.sum(
            jnp.dot(hidden_one, dir_bf16, preferred_element_type=jnp.float32) * slope_out, axis=-1
        )
        return lax.psum(partial_rows, "mp")

    gradient = lax.psum(pull_back(hidden_one, grad_back), "dp")

    def spread(vector):
        return vector.astype(jnp.bfloat16)

    def inner_product(first, second):
        return lax.psum(jnp.sum(first * second), "mp")

    solution = jnp.zeros_like(gradient)
    remainder = -gradient
    direction = remainder
    norm_now = inner_product(remainder, remainder)
    for iteration in range(ITERS):
        summed = lax.psum(
            pull_back(
                hidden_one,
                ((row_weight * tangent(spread(direction)))[:, None] * slope_out).astype(
                    jnp.bfloat16
                ),
            ),
            "dp",
        )
        curved = summed + damping * direction
        step_size = norm_now / inner_product(direction, curved)
        solution = solution + step_size * direction
        remainder = remainder - step_size * curved
        if iteration + 1 < ITERS:
            norm_next = inner_product(remainder, remainder)
            direction = remainder + norm_next / norm_now * direction
            norm_now = norm_next
    return tangent(spread(solution))


def solution(mesh):
    return jax.shard_map(
        shards,
        mesh=mesh,
        in_specs=(P(None, "dp"), P(None, "mp"), P(None, "mp"), P("mp"), P("dp"), P("dp")),
        out_specs=P("dp"),
        check_vma=False,
    )
```

profile of v0, /device:TPU:0, one launch (start us, length us, event | category | flops | bytes accessed | tf_op | source)
XLA Modules:
  0.0 518.2 jit_solution(10270129785186823184)
XLA Ops:
  8.5 23.6 %psum.112 = f32[]{:T(128)} all-reduce(f32[]{:T(128)S(6)} %convert_element_type.36), channel_id=1, replica_groups=mesh['dp'=8,'mp'=4] {'dp'}, use_global_device_ids=true, to_apply=%region_1.0 | all-reduce | flops 1 | bytes 8 | tf_op jit(solution)/shard_map/psum | solution.py:19
  34.3 5.4 %all_gather.3 = bf16[16,1024]{1,0:T(8,128)(2,1)S(1)} all-gather(bf16[16,256]{1,0:T(8,128)(2,1)} %param.7), channel_id=1, replica_groups=mesh['dp'=8,'mp'=4] {'mp'}, dimensions={1}, use_global_device_ids=true | all-gather | bytes 40960 | tf_op jit(solution)/shard_map/all_gather | solution.py:20
  46.3 11.3 %psum.113 = f32[3072]{0:T(1024)S(1)} all-reduce(f32[3072]{0:T(1024)S(1)} %get-tuple-element.11), channel_id=1, replica_groups=mesh['dp'=8,'mp'=4] {'mp'}, use_global_device_ids=true, to_apply=%region_3.0 | all-reduce | flops 3072 | bytes 24576 | tf_op jit(solution)/shard_map/psum | solution.py:26
  57.6 6.7 %fusion = f32[1024,256]{1,0:T(8,128)} fusion(bf16[3072,1024]{1,0:T(8,128)(2,1)} %copy-done.1, f32[3072]{0:T(1024)S(1)} %subtract_multiply_fusion.1, f32[3072,256]{0,1:T(8,128)} %get-tuple-element.12, f32[256]{0:T(256)S(1)} %convert_element_type.37), kind=kOutput, calls=%fused_computation.12 | convolution fusion | flops 1614544896 | bytes 10499072 | tf_op jit(solution)/shard_map/dot_general | solution.py:12
  64.4 74.4 %all-reduce.6.cloned.1.call-done = f32[1024,256]{1,0:T(8,128)} async-done(((f32[1024,256]{1,0:T(8,128)}), f32[1024,256]{1,0:T(8,128)}) %all-reduce.6.cloned.1.call-update) | async-done | bytes 1048592 | tf_op jit(solution)/shard_map/psum | solution.py:42
  138.8 6.2 %fusion.8 = f32[3072]{0:T(1024)S(1)} fusion(bf16[3072,1024]{1,0:T(8,128)(2,1)} %copy-done.1, f32[1024,256]{1,0:T(8,128)} %all-reduce.6.cloned.1.call-done, f32[256]{0:T(256)S(1)} %convert_element_type.37, f32[3072,256]{0,1:T(8,128)} %get-tuple-element.12), kind=kOutput, calls=%fused_computation.20 | convolution fusion | flops 1615066112 | bytes 10499072 | tf_op jit(solution)/shard_map/dot_general | solution.py:38
  145.0 10.2 %psum.116 = f32[3072]{0:T(1024)S(1)} all-reduce(f32[3072]{0:T(1024)S(1)} %fusion.8), channel_id=1, replica_groups=mesh['dp'=8,'mp'=4] {'mp'}, use_global_device_ids=true, to_apply=%region_8.0 | all-reduce | flops 3072 | bytes 24576 | tf_op jit(solution)/shard_map/psum | solution.py:40
  155.2 6.8 %fusion.1 = f32[1024,256]{1,0:T(8,128)} fusion(bf16[3072,1024]{1,0:T(8,128)(2,1)} %copy-done.1, f32[3072]{0:T(1024)S(1)} %mul.147, f32[3072,256]{0,1:T(8,128)} %get-tuple-element.12, f32[256]{0:T(256)S(1)} %convert_element_type.37), kind=kOutput, calls=%fused_computation.13 | convolution fusion | flops 1614544896 | bytes 10499072 | tf_op jit(solution)/shard_map/dot_general | solution.py:12
  162.2 77.6 %all-reduce.8.cloned.1.call-done = f32[1024,256]{1,0:T(8,128)} async-done(((f32[1024,256]{1,0:T(8,128)}), f32[1024,256]{1,0:T(8,128)}) %all-reduce.8.cloned.1.call-update) | async-done | bytes 1048592 | tf_op jit(solution)/shard_map/psum | solution.py:55
  242.0 6.5 %all-reduce = (f32[]{:T(128)}, f32[]{:T(128)}) all-reduce(f32[]{:T(128)} %get-tuple-element.6, f32[]{:T(128)} %get-tuple-element.5), channel_id=1, replica_groups=mesh['dp'=8,'mp'=4] {'mp'}, use_global_device_ids=true, to_apply=%region_6.0 | all-reduce | flops 2 | bytes 16 | tf_op jit(solution)/shard_map/psum | solution.py:48
  251.9 7.0 %psum.119 = f32[]{:T(128)} all-reduce(f32[]{:T(128)} %get-tuple-element.9), channel_id=1, replica_groups=mesh['dp'=8,'mp'=4] {'mp'}, use_global_device_ids=true, to_apply=%region_13.0 | all-reduce | flops 1 | bytes 8 | tf_op jit(solution)/shard_map/psum | solution.py:48
  262.4 5.1 fusion.9
  267.6 10.2 %psum.120 = f32[3072]{0:T(1024)S(1)} all-reduce(f32[3072]{0:T(1024)S(1)} %fusion.9), channel_id=1, replica_groups=mesh['dp'=8,'mp'=4] {'mp'}, use_global_device_ids=true, to_apply=%region_15.0 | all-reduce | flops 3072 | bytes 24576 | tf_op jit(solution)/shard_map/psum | solution.py:40
  277.8 6.7 %fusion.2 = f32[1024,256]{1,0:T(8,128)} fusion(bf16[3072,1024]{1,0:T(8,128)(2,1)} %copy-done.1, f32[3072]{0:T(1024)S(1)} %mul.159, f32[3072,256]{0,1:T(8,128)} %get-tuple-element.12, f32[256]{0:T(256)S(1)} %convert_element_type.37), kind=kOutput, calls=%fused_computation.14 | convolution fusion | flops 1614544896 | bytes 10499072 | tf_op jit(solution)/shard_map/dot_general | solution.py:12
  284.6 77.0 %all-reduce.10.cloned.1.call-done = f32[1024,256]{1,0:T(8,128)} async-done(((f32[1024,256]{1,0:T(8,128)}), f32[1024,256]{1,0:T(8,128)}) %all-reduce.10.cloned.1.call-update) | async-done | bytes 1048592 | tf_op jit(solution)/shard_map/psum | solution.py:55
  363.7 6.5 %psum.122 = f32[]{:T(128)} all-reduce(f32[]{:T(128)} %multiply_reduce_fusion.3), channel_id=1, replica_groups=mesh['dp'=8,'mp'=4] {'mp'}, use_global_device_ids=true, to_apply=%region_18.0 | all-reduce | flops 1 | bytes 8 | tf_op jit(solution)/shard_map/psum | solution.py:48
  373.6 7.0 %psum.123 = f32[]{:T(128)} all-reduce(f32[]{:T(128)} %multiply_reduce_fusion.2), channel_id=1, replica_groups=mesh['dp'=8,'mp'=4] {'mp'}, use_global_device_ids=true, to_apply=%region_20.0 | all-reduce | flops 1 | bytes 8 | tf_op jit(solution)/shard_map/psum | solution.py:48
  384.5 5.2 fusion.10
  389.6 10.2 %psum.124 = f32[3072]{0:T(1024)S(1)} all-reduce(f32[3072]{0:T(1024)S(1)} %fusion.10), channel_id=1, replica_groups=mesh['dp'=8,'mp'=4] {'mp'}, use_global_device_ids=true, to_apply=%region_22.0 | all-reduce | flops 3072 | bytes 24576 | tf_op jit(solution)/shard_map/psum | solution.py:40
  399.8 6.8 %fusion.3 = f32[1024,256]{1,0:T(8,128)} fusion(bf16[3072,1024]{1,0:T(8,128)(2,1)} %copy-done.1, f32[3072]{0:T(1024)S(1)} %mul.171, f32[3072,256]{0,1:T(8,128)} %get-tuple-element.12, f32[256]{0:T(256)S(1)} %convert_element_type.37), kind=kOutput, calls=%fused_computation.15 | convolution fusion | flops 1614544896 | bytes 10499072 | tf_op jit(solution)/shard_map/dot_general | solution.py:12
  406.7 77.1 %all-reduce.12.cloned.1.call-done = f32[1024,256]{1,0:T(8,128)} async-done(((f32[1024,256]{1,0:T(8,128)}), f32[1024,256]{1,0:T(8,128)}) %all-reduce.12.cloned.1.call-update) | async-done | bytes 1048592 | tf_op jit(solution)/shard_map/psum | solution.py:55
  486.2 6.7 %psum.126 = f32[]{:T(128)} all-reduce(f32[]{:T(128)} %multiply_reduce_fusion.1), channel_id=1, replica_groups=mesh['dp'=8,'mp'=4] {'mp'}, use_global_device_ids=true, to_apply=%region_25.0 | all-reduce | flops 1 | bytes 8 | tf_op jit(solution)/shard_map/psum | solution.py:48
  494.1 6.3 %fusion.11 = f32[3072]{0:T(1024)S(1)} fusion(bf16[3072,1024]{1,0:T(8,128)(2,1)} %copy-done.1, f32[1024,256]{1,0:T(8,128)} %copy-done.4, f32[1024,256]{1,0:T(8,128)S(1)} %multiply_add_fusion.2, f32[1024,256]{1,0:T(8,128)S(1)} %copy-done.3, f32[]{:T(128)S(6)} %div.30, f32[]{:T(128)S(6)} %div.28, f32[]{:T(128)S(6)} %div.26, f32[256]{0:T(256)S(1)} %convert_element_type.37, ...), kind=kOutput, calls=%fused_computation.23 | convolution fusion | flops 1616376832 | bytes 12596236 | tf_op jit(solution)/shard_map/dot_general | solution.py:38
  500.4 11.2 %psum.127 = f32[3072]{0:T(1024)} all-reduce(f32[3072]{0:T(1024)S(1)} %fusion.11), channel_id=1, replica_groups=mesh['dp'=8,'mp'=4] {'mp'}, use_global_device_ids=true, to_apply=%region_27.0 | all-reduce | flops 3072 | bytes 24576 | tf_op jit(solution)/shard_map/psum | solution.py:40
  (41 shorter events, 25.4 us)
Async XLA Ops:
  6.5 35.9 %copy-start = (bf16[1024,256]{1,0:T(8,128)(2,1)S(1)}, bf16[1024,256]{1,0:T(8,128)(2,1)}, u32[]{:S(2)}) copy-start(bf16[1024,256]{1,0:T(8,128)(2,1)} %param.8) | copy-start | bytes 1572868
  6.5 132.2 %all-reduce.6.cloned.1.call-start = ((), (), s32[]{:S(2)}) async-start(), calls=%async_computation | async-start | bytes 2097152 | tf_op jit(solution)/shard_map/psum | solution.py:42
  42.5 3.8 copy-start.1
  42.5 15.1 %copy-start.5 = (f32[3072]{0:T(1024)S(1)}, f32[3072]{0:T(1024)}, u32[]{:S(2)}) copy-start(f32[3072]{0:T(1024)} %param.10) | copy-start | bytes 36868
  64.3 175.5 %all-reduce.8.cloned.1.call-start = ((), (), s32[]{:S(2)}) async-start(), calls=%async_computation.1 | async-start | bytes 2097152 | tf_op jit(solution)/shard_map/psum | solution.py:55
  155.2 84.7 %copy-start.2 = (f32[1024,256]{1,0:T(8,128)S(1)}, f32[1024,256]{1,0:T(8,128)}, u32[]{:S(2)}) copy-start(f32[1024,256]{1,0:T(8,128)} %all-reduce.6.cloned.1.call-done) | copy-start | bytes 3145732
  162.0 199.6 %all-reduce.10.cloned.1.call-start = ((), (), s32[]{:S(2)}) async-start(), calls=%async_computation.2 | async-start | bytes 2097152 | tf_op jit(solution)/shard_map/psum | solution.py:55
  260.2 2.2 copy-start.6
  284.5 199.2 %all-reduce.12.cloned.1.call-start = ((), (), s32[]{:S(2)}) async-start(), calls=%async_computation.3 | async-start | bytes 2097152 | tf_op jit(solution)/shard_map/psum | solution.py:55
  381.9 2.6 copy-start.7
  383.5 1.0 copy-start.4
  406.6 87.5 %copy-start.3 = (f32[1024,256]{1,0:T(8,128)S(1)}, f32[1024,256]{1,0:T(8,128)}, u32[]{:S(2)}) copy-start(f32[1024,256]{1,0:T(8,128)} %all-reduce.6.cloned.1.call-done) | copy-start | bytes 3145732
Sparse Core Ops, SparseCore 0:
  64.5 74.2 all-reduce.5
  162.1 77.7 all-reduce.7
  284.6 76.9 all-reduce.9
  406.8 76.9 all-reduce.11
where the time goes:
time: 519 us; the launch traced here: 518 us
  waiting for transfers between devices  306 us (59%)
  blocking collectives  116 us (22%)
  matrix products  56.2 us (11%)
  between operations  21 us (4%)
  other arithmetic  16.8 us (3%)
    psum x3, waiting for transfers between devices, shards(): lax.psum(pull_back(hidden_one, ((row_weight * tangent(spread(direction)))...  232 us
    psum x1, waiting for transfers between devices, shards(): gradient = lax.psum(pull_back(hidden_one, grad_back), 'dp')  74.4 us
    psum x4, blocking collectives, tangent(): return lax.psum(partial_rows, 'mp')  41.8 us
    psum x5, blocking collectives, inner_product(): return lax.psum(jnp.sum(first * second), 'mp')  33.7 us
    dot_general x4, matrix products, pull_back(): lax.dot_general(columns, back, (((0,), (0,)), ((), ())), preferred_elemen...  27 us
    psum x1, blocking collectives, shards(): valid_count = lax.psum(jnp.sum(valid_steps).astype(jnp.float32), 'dp')  23.6 us
    dot_general x4, matrix products, tangent(): jnp.dot(hidden_one, dir_bf16, preferred_element_type=jnp.float32)  22.8 us
    psum x1, blocking collectives, shards(): predicted = lax.psum(jnp.sum(hidden_two * out_weight, axis=-1), 'mp')  11.3 us
  transfers between devices with their start and end apart: 4, of which 4 were waited for; matrix products, arithmetic and copies ran while one was open for 0% of the time, Pallas kernels for 0%

commit v1 on v0

--- a/solution.py
+++ b/solution.py
@@ -39,7 +39,9 @@
         )
         return lax.psum(partial_rows, "mp")
 
-    gradient = lax.psum(pull_back(hidden_one, grad_back), "dp")
+    block = pull_back(hidden_one, grad_back)
+    parts = lax.all_gather(block, "dp")
+    gradient = jnp.sum(parts, axis=0)
 
     def spread(vector):
         return vector.astype(jnp.bfloat16)

time: 519 us -> 569 us (1.096)
  waiting for transfers between devices: 306 us -> 351 us
    all_gather x0 -> x1, waiting for transfers between devices: none -> 121 us  [shards(): parts = lax.all_gather(block, 'dp')]
    psum x1 -> x0, waiting for transfers between devices: 74.4 us -> none  [shards(): gradient = lax.psum(pull_back(hidden_one, grad_back), 'dp')]
where the time goes in v1:
time: 569 us; the launch traced here: 568 us
  waiting for transfers between devices  351 us (62%)
  blocking collectives  116 us (20%)
  matrix products  56.2 us (10%)
  between operations  21.2 us (4%)
  other arithmetic  20.8 us (4%)
    psum x3, waiting for transfers between devices, shards(): lax.psum(pull_back(hidden_one, ((row_weight * tangent(spread(direction)))...  230 us
    all_gather x1, waiting for transfers between devices, shards(): parts = lax.all_gather(block, 'dp')  121 us
    psum x4, blocking collectives, tangent(): return lax.psum(partial_rows, 'mp')  42.5 us
    psum x5, blocking collectives, inner_product(): return lax.psum(jnp.sum(first * second), 'mp')  33.4 us
    dot_general x4, matrix products, pull_back(): lax.dot_general(columns, back, (((0,), (0,)), ((), ())), preferred_elemen...  26.9 us
    psum x1, blocking collectives, shards(): valid_count = lax.psum(jnp.sum(valid_steps).astype(jnp.float32), 'dp')  23.6 us
    dot_general x4, matrix products, tangent(): jnp.dot(hidden_one, dir_bf16, preferred_element_type=jnp.float32)  22.8 us
  transfers between devices with their start and end apart: 4, of which 4 were waited for; matrix products, arithmetic and copies ran while one was open for 0% of the time, Pallas kernels for 0%

profile of v1, /device:TPU:0, one launch (start us, length us, event | category | flops | bytes accessed | tf_op | source)
XLA Modules:
  0.0 567.8 jit_solution(7623745669956723177)
XLA Ops:
  8.5 23.6 %psum.105 = f32[]{:T(128)} all-reduce(f32[]{:T(128)S(6)} %convert_element_type.36), channel_id=1, replica_groups=mesh['dp'=8,'mp'=4] {'dp'}, use_global_device_ids=true, to_apply=%region_1.0 | all-reduce | flops 1 | bytes 8 | tf_op jit(solution)/shard_map/psum | solution.py:19
  34.3 5.4 all_gather.9
  46.2 11.3 %psum.106 = f32[3072]{0:T(1024)S(1)} all-reduce(f32[3072]{0:T(1024)S(1)} %get-tuple-element.11), channel_id=1, replica_groups=mesh['dp'=8,'mp'=4] {'mp'}, use_global_device_ids=true, to_apply=%region_3.0 | all-reduce | flops 3072 | bytes 24576 | tf_op jit(solution)/shard_map/psum | solution.py:26
  57.5 6.8 %fusion = f32[1024,256]{1,0:T(8,128)} fusion(bf16[3072,1024]{1,0:T(8,128)(2,1)} %copy-done.1, f32[3072]{0:T(1024)S(1)} %subtract_multiply_fusion.1, f32[3072,256]{0,1:T(8,128)} %get-tuple-element.12, f32[256]{0:T(256)S(1)} %convert_element_type.37), kind=kOutput, calls=%fused_computation.12 | convolution fusion | flops 1614544896 | bytes 10499072 | tf_op jit(solution)/shard_map/dot_general | solution.py:12
  64.4 121.3 %all-gather.3.cloned.1.call-done = f32[8192,256]{1,0:T(8,128)} async-done(((f32[1024,256]{1,0:T(8,128)}), f32[8192,256]{1,0:T(8,128)}) %all-gather.3.cloned.1.call-update) | async-done | bytes 8388624 | tf_op jit(solution)/shard_map/all_gather | solution.py:43
  189.8 6.3 %fusion.8 = f32[3072]{0:T(1024)S(1)} fusion(bf16[3072,1024]{1,0:T(8,128)(2,1)} %copy-done.1, f32[1024,256]{1,0:T(8,128)S(1)} %reduce_sum.119, f32[256]{0:T(256)S(1)} %convert_element_type.37, f32[3072,256]{0,1:T(8,128)} %get-tuple-element.12), kind=kOutput, calls=%fused_computation.20 | convolution fusion | flops 1615066112 | bytes 10499072 | tf_op jit(solution)/shard_map/dot_general | solution.py:38
  196.1 10.4 %psum.108 = f32[3072]{0:T(1024)S(1)} all-reduce(f32[3072]{0:T(1024)S(1)} %fusion.8), channel_id=1, replica_groups=mesh['dp'=8,'mp'=4] {'mp'}, use_global_device_ids=true, to_apply=%region_8.0 | all-reduce | flops 3072 | bytes 24576 | tf_op jit(solution)/shard_map/psum | solution.py:40
  206.5 6.7 %fusion.1 = f32[1024,256]{1,0:T(8,128)} fusion(bf16[3072,1024]{1,0:T(8,128)(2,1)} %copy-done.1, f32[3072]{0:T(1024)S(1)} %mul.147, f32[3072,256]{0,1:T(8,128)} %get-tuple-element.12, f32[256]{0:T(256)S(1)} %convert_element_type.37), kind=kOutput, calls=%fused_computation.13 | convolution fusion | flops 1614544896 | bytes 10499072 | tf_op jit(solution)/shard_map/dot_general | solution.py:12
  213.3 76.1 %all-reduce.5.cloned.1.call-done = f32[1024,256]{1,0:T(8,128)} async-done(((f32[1024,256]{1,0:T(8,128)}), f32[1024,256]{1,0:T(8,128)}) %all-reduce.5.cloned.1.call-update) | async-done | bytes 1048592 | tf_op jit(solution)/shard_map/psum | solution.py:57
  291.6 6.5 %all-reduce = (f32[]{:T(128)}, f32[]{:T(128)}) all-reduce(f32[]{:T(128)} %get-tuple-element.6, f32[]{:T(128)} %get-tuple-element.5), channel_id=1, replica_groups=mesh['dp'=8,'mp'=4] {'mp'}, use_global_device_ids=true, to_apply=%region_6.0 | all-reduce | flops 2 | bytes 16 | tf_op jit(solution)/shard_map/psum | solution.py:50
  301.5 7.0 %psum.111 = f32[]{:T(128)} all-reduce(f32[]{:T(128)} %get-tuple-element.9), channel_id=1, replica_groups=mesh['dp'=8,'mp'=4] {'mp'}, use_global_device_ids=true, to_apply=%region_13.0 | all-reduce | flops 1 | bytes 8 | tf_op jit(solution)/shard_map/psum | solution.py:50
  312.0 5.1 fusion.9
  317.1 10.2 %psum.112 = f32[3072]{0:T(1024)S(1)} all-reduce(f32[3072]{0:T(1024)S(1)} %fusion.9), channel_id=1, replica_groups=mesh['dp'=8,'mp'=4] {'mp'}, use_global_device_ids=true, to_apply=%region_15.0 | all-reduce | flops 3072 | bytes 24576 | tf_op jit(solution)/shard_map/psum | solution.py:40
  327.3 6.7 %fusion.2 = f32[1024,256]{1,0:T(8,128)} fusion(bf16[3072,1024]{1,0:T(8,128)(2,1)} %copy-done.1, f32[3072]{0:T(1024)S(1)} %mul.159, f32[3072,256]{0,1:T(8,128)} %get-tuple-element.12, f32[256]{0:T(256)S(1)} %convert_element_type.37), kind=kOutput, calls=%fused_computation.14 | convolution fusion | flops 1614544896 | bytes 10499072 | tf_op jit(solution)/shard_map/dot_general | solution.py:12
  334.1 77.1 %all-reduce.7.cloned.1.call-done = f32[1024,256]{1,0:T(8,128)} async-done(((f32[1024,256]{1,0:T(8,128)}), f32[1024,256]{1,0:T(8,128)}) %all-reduce.7.cloned.1.call-update) | async-done | bytes 1048592 | tf_op jit(solution)/shard_map/psum | solution.py:57
  413.3 6.5 %psum.114 = f32[]{:T(128)} all-reduce(f32[]{:T(128)} %multiply_reduce_fusion.3), channel_id=1, replica_groups=mesh['dp'=8,'mp'=4] {'mp'}, use_global_device_ids=true, to_apply=%region_18.0 | all-reduce | flops 1 | bytes 8 | tf_op jit(solution)/shard_map/psum | solution.py:50
  423.2 7.0 %psum.115 = f32[]{:T(128)} all-reduce(f32[]{:T(128)} %multiply_reduce_fusion.2), channel_id=1, replica_groups=mesh['dp'=8,'mp'=4] {'mp'}, use_global_device_ids=true, to_apply=%region_20.0 | all-reduce | flops 1 | bytes 8 | tf_op jit(solution)/shard_map/psum | solution.py:50
  434.1 5.2 fusion.10
  439.3 10.7 %psum.116 = f32[3072]{0:T(1024)S(1)} all-reduce(f32[3072]{0:T(1024)S(1)} %fusion.10), channel_id=1, replica_groups=mesh['dp'=8,'mp'=4] {'mp'}, use_global_device_ids=true, to_apply=%region_22.0 | all-reduce | flops 3072 | bytes 24576 | tf_op jit(solution)/shard_map/psum | solution.py:40
  450.0 6.7 %fusion.3 = f32[1024,256]{1,0:T(8,128)} fusion(bf16[3072,1024]{1,0:T(8,128)(2,1)} %copy-done.1, f32[3072]{0:T(1024)S(1)} %mul.171, f32[3072,256]{0,1:T(8,128)} %get-tuple-element.12, f32[256]{0:T(256)S(1)} %convert_element_type.37), kind=kOutput, calls=%fused_computation.15 | convolution fusion | flops 1614544896 | bytes 10499072 | tf_op jit(solution)/shard_map/dot_general | solution.py:12
  456.7 76.9 %all-reduce.9.cloned.1.call-done = f32[1024,256]{1,0:T(8,128)} async-done(((f32[1024,256]{1,0:T(8,128)}), f32[1024,256]{1,0:T(8,128)}) %all-reduce.9.cloned.1.call-update) | async-done | bytes 1048592 | tf_op jit(solution)/shard_map/psum | solution.py:57
  536.0 6.5 %psum.118 = f32[]{:T(128)} all-reduce(f32[]{:T(128)} %multiply_reduce_fusion.1), channel_id=1, replica_groups=mesh['dp'=8,'mp'=4] {'mp'}, use_global_device_ids=true, to_apply=%region_25.0 | all-reduce | flops 1 | bytes 8 | tf_op jit(solution)/shard_map/psum | solution.py:50
  543.8 6.3 %fusion.11 = f32[3072]{0:T(1024)S(1)} fusion(bf16[3072,1024]{1,0:T(8,128)(2,1)} %copy-done.1, f32[1024,256]{1,0:T(8,128)} %copy-done.4, f32[1024,256]{1,0:T(8,128)S(1)} %multiply_add_fusion.2, f32[1024,256]{1,0:T(8,128)S(1)} %copy-done.3, f32[]{:T(128)S(6)} %div.30, f32[]{:T(128)S(6)} %div.28, f32[]{:T(128)S(6)} %div.26, f32[256]{0:T(256)S(1)} %convert_element_type.37, ...), kind=kOutput, calls=%fused_computation.23 | convolution fusion | flops 1616376832 | bytes 12596236 | tf_op jit(solution)/shard_map/dot_general | solution.py:38
  550.0 11.2 %psum.119 = f32[3072]{0:T(1024)} all-reduce(f32[3072]{0:T(1024)S(1)} %fusion.11), channel_id=1, replica_groups=mesh['dp'=8,'mp'=4] {'mp'}, use_global_device_ids=true, to_apply=%region_27.0 | all-reduce | flops 3072 | bytes 24576 | tf_op jit(solution)/shard_map/psum | solution.py:40
  (42 shorter events, 29.2 us)
Async XLA Ops:
  6.5 35.9 %copy-start = (bf16[1024,256]{1,0:T(8,128)(2,1)S(1)}, bf16[1024,256]{1,0:T(8,128)(2,1)}, u32[]{:S(2)}) copy-start(bf16[1024,256]{1,0:T(8,128)(2,1)} %param.8) | copy-start | bytes 1572868
  6.5 179.2 %all-gather.3.cloned.1.call-start = ((), (), s32[]{:S(2)}) async-start(), calls=%async_computation.3 | async-start | bytes 9437184 | tf_op jit(solution)/shard_map/all_gather | solution.py:43
  42.5 3.7 copy-start.1
  42.5 15.0 %copy-start.5 = (f32[3072]{0:T(1024)S(1)}, f32[3072]{0:T(1024)}, u32[]{:S(2)}) copy-start(f32[3072]{0:T(1024)} %param.10) | copy-start | bytes 36868
  64.3 225.1 %all-reduce.5.cloned.1.call-start = ((), (), s32[]{:S(2)}) async-start(), calls=%async_computation | async-start | bytes 2097152 | tf_op jit(solution)/shard_map/psum | solution.py:57
  189.8 109.6 %copy-start.2 = (f32[1024,256]{1,0:T(8,128)}, f32[1024,256]{1,0:T(8,128)S(1)}, u32[]{:S(2)}) copy-start(f32[1024,256]{1,0:T(8,128)S(1)} %reduce_sum.119) | copy-start | bytes 3145732
  213.3 197.9 %all-reduce.7.cloned.1.call-start = ((), (), s32[]{:S(2)}) async-start(), calls=%async_computation.1 | async-start | bytes 2097152 | tf_op jit(solution)/shard_map/psum | solution.py:57
  309.8 2.2 copy-start.6
  334.1 199.5 %all-reduce.9.cloned.1.call-start = ((), (), s32[]{:S(2)}) async-start(), calls=%async_computation.2 | async-start | bytes 2097152 | tf_op jit(solution)/shard_map/psum | solution.py:57
  431.5 2.6 copy-start.7
  433.1 1.0 copy-start.4
  456.7 87.1 %copy-start.3 = (f32[1024,256]{1,0:T(8,128)S(1)}, f32[1024,256]{1,0:T(8,128)}, u32[]{:S(2)}) copy-start(f32[1024,256]{1,0:T(8,128)} %copy-done.2) | copy-start | bytes 3145732
Sparse Core Ops, SparseCore 0:
  64.4 121.2 all-gather.2
  213.4 75.9 all-reduce.4
  334.2 76.9 all-reduce.6
  456.8 76.6 all-reduce.8
